TPU v7x, 32 devices: a whole 2x2x4 slice. The times are simulated.
32 devices in a mesh: groups: 2 (over x), op: 16 (over z, y, core).
Axes of the slice: x: 2, y: 2, z: 4, core: 2. Of those that a mesh axis runs over, the one named last changes fastest.
Arguments:
- wavefunction: bfloat16 [256, 3, 128, 128], P(('groups', 'op')), parts along dimension 0, as said below
- left_env: bfloat16 [64, 128, 128, 128], P(('groups', 'op')), parts along dimension 0, as said below
- right_env: bfloat16 [64, 128, 128, 128], P(('groups', 'op')), parts along dimension 0, as said below
- term_shift: int32 [64], P('groups'), parts along dimension 0, may hold values from 0 to 2
- sector_width: int32 [256], P(('groups', 'op')), parts along dimension 0, may hold values from 1 to 128, as said below
Outputs:
- sigma_out: float32 [256, 3, 128, 128], P(('groups', 'op')), parts along dimension 0
There are 2 independent parts, one for each index of `groups`. A program takes and returns all parts, laid end to end along the dimension named above; each array names one. Nothing has to cross between parts.
Inputs may be any that keep to these rules, and one draw needn't show every extreme that they name: `sector_width`: sector widths sum to 12288 and exactly one sector has width 128. `wavefunction`: rows and columns at or past a sector's width are zero in that sector's blocks. `left_env`: rows at or past a sector's width are zero in that sector's blocks. `right_env`: rows at or past a sector's width are zero in that sector's blocks.
All inputs are finite; a program needn't handle non-finite values.
Results may differ from a plain program's by a relative error of at most 0.0029.
Values may be sent and summed in bfloat16 or wider, within the bound.
A program may use at most 192 MiB of HBM per device.

v0:
```python
import jax
import jax.numpy as jnp
from jax import lax
from jax.sharding import PartitionSpec as P

TERMS = 32


def per_device(wavefunction, left_env, right_env, term_shift, sector_width):
    devices = lax.axis_size("op")
    split_count = max(1, devices // TERMS)
    slot_dev = left_env.shape[0]
    half_sec = left_env.shape[1]
    block_tail = wavefunction.shape[1:]
    gathered = lax.all_gather(wavefunction, "op", axis=0, tiled=True)
    zero_block = jnp.zeros((1,) + block_tail, gathered.dtype)
    padded = jnp.concatenate([zero_block, gathered, zero_block], axis=0)
    my_index = lax.axis_index("op")
    places = jnp.arange(half_sec, dtype=jnp.int32)
    partial_value = jnp.zeros((half_sec,) + block_tail, jnp.float32)
    for slot_index in range(slot_dev):
        slot_rank = my_index * slot_dev + slot_index
        half_index = slot_rank // TERMS
        term_index = slot_rank % TERMS
        shift_value = term_shift[term_index] - 1
        row_index = places * split_count + half_index - shift_value + 1
        source = jnp.take(padded, row_index, axis=0)
        inner_block = jnp.einsum(
            "qij,qvjk->qvik", left_env[slot_index], source, preferred_element_type=jnp.float32
        ).astype(jnp.bfloat16)
        partial_value = partial_value + jnp.einsum(
            "qvik,qlk->qvil", inner_block, right_env[slot_index], preferred_element_type=jnp.float32
        )
    arrived = lax.all_to_all(partial_value, "op", split_axis=0, concat_axis=0, tiled=True)
    per_peer = half_sec // devices
    grouped = arrived.reshape((split_count, devices // split_count, per_peer) + block_tail)
    summed = jnp.sum(grouped, axis=1)
    summed = jnp.swapaxes(summed, 0, 1).reshape(wavefunction.shape)
    line_index = jnp.arange(wavefunction.shape[2], dtype=jnp.int32)
    widths = sector_width[:, None, None]
    keep_mask = (line_index[None, :, None] < widths) & (line_index[None, None, :] < widths)
    return jnp.where(keep_mask[:, None], summed, jnp.float32(0.0))


def solution(mesh):
    return jax.shard_map(
        per_device,
        mesh=mesh,
        in_specs=(
            P(("groups", "op"), None, None, None),
            P(("groups", "op"), None, None, None),
            P(("groups", "op"), None, None, None),
            P("groups"),
            P(("groups", "op")),
        ),
        out_specs=P(("groups", "op"), None, None, None),
        check_vma=False,
    )
```

profile of v0, /device:TPU:13, one launch (start us, length us, event | category | flops | bytes accessed | tf_op | source)
XLA Modules:
  0.0 757.4 jit_solution(12843564471308969780)
XLA Ops:
  6.5 0.0 all-gather.2.cloned.1.call-start
  6.5 0.7 all-gather.2.cloned.1.call-update
  7.3 1.4 fusion.45
  10.1 99.6 %all-gather.2.cloned.1.call-done = bf16[128,3,128,128]{3,2,1,0:T(8,128)(2,1)} async-done(((bf16[8,3,128,128]{3,2,1,0:T(8,128)(2,1)}), bf16[128,3,128,128]{3,2,1,0:T(8,128)(2,1)}) %all-gather.2.cloned.1.call-update) | async-done | bytes 12582928 | tf_op jit(solution)/shard_map/all_gather | solution.py:15
  109.7 11.1 %pad_maximum_fusion = bf16[130,3,128,128]{3,2,1,0:T(8,128)(2,1)} fusion(bf16[1,3,128,128]{3,2,1,0:T(8,128)(2,1)S(1)} %broadcast_in_dim.29, bf16[128,3,128,128]{3,2,1,0:T(8,128)(2,1)} %all-gather.2.cloned.1.call-done), kind=kLoop, calls=%fused_computation.2 | loop fusion | flops 12779520 | bytes 25460736 | tf_op jit(solution)/shard_map/concatenate | solution.py:17
  120.8 13.0 %gather_fusion.1 = bf16[128,3,128,128]{3,2,1,0:T(8,128)(2,1)} fusion(bf16[130,3,128,128]{3,2,1,0:T(8,128)(2,1)} %pad_maximum_fusion, s32[1024]{0:T(1024)S(1)} %pad_clamp_fusion), kind=kCustom, calls=%fused_computation.1.clone | custom fusion | bytes 25166336 | tf_op jit(solution)/shard_map/jit(_take)/gather | solution.py:27
  133.8 13.1 %gather_fusion = bf16[128,3,128,128]{3,2,1,0:T(8,128)(2,1)} fusion(bf16[130,3,128,128]{3,2,1,0:T(8,128)(2,1)} %pad_maximum_fusion, s32[1024]{0:T(1024)S(1)} %pad_clamp_fusion.1), kind=kCustom, calls=%fused_computation.clone | custom fusion | bytes 25166336 | tf_op jit(solution)/shard_map/jit(_take)/gather | solution.py:27
  146.9 19.1 %fusion = f32[128,3,128,128]{3,2,1,0:T(8,128)} fusion(bf16[128,3,128,128]{3,2,1,0:T(8,128)(2,1)} %gather_fusion.1, pred[128]{0:T(512)(128)(4,1)S(1)} %get-tuple-element.8, bf16[2,128,128,128]{3,2,1,0:T(8,128)(2,1)} %param.9, bf16[2,128,128,128]{3,2,1,0:T(8,128)(2,1)} %param.8), kind=kOutput, calls=%fused_computation.3 | convolution fusion | flops 3233808384 | bytes 46137472 | tf_op jit(solution)/shard_map/qvik,qlk->qvil/dot_general | solution.py:31
  166.0 24.1 %fusion.24 = f32[128,3,128,128]{3,2,1,0:T(8,128)} fusion(f32[128,3,128,128]{3,2,1,0:T(8,128)} %fusion, bf16[128,3,128,128]{3,2,1,0:T(8,128)(2,1)} %gather_fusion, pred[128]{0:T(512)(128)(4,1)S(1)} %get-tuple-element.6, bf16[2,128,128,128]{3,2,1,0:T(8,128)(2,1)} %param.9, bf16[2,128,128,128]{3,2,1,0:T(8,128)(2,1)} %param.8), kind=kOutput, calls=%fused_computation.17 | convolution fusion | flops 3240099840 | bytes 71303296 | tf_op jit(solution)/shard_map/qvik,qlk->qvil/dot_general | solution.py:31
  190.1 0.0 copy-start
  190.1 8.1 %all-to-all-start = ((f32[128,3,128,128]{3,2,1,0:T(8,128)}), f32[128,3,128,128]{3,2,1,0:T(8,128)}, u32[]{:S(2)}, u32[]{:S(2)}) async-start(f32[128,3,128,128]{3,2,1,0:T(8,128)} %fusion.24), calls=%async_computation | async-start | bytes 50331648 | tf_op jit(solution)/shard_map/all_to_all | solution.py:34
  198.2 0.0 copy-done
  198.2 0.1 iota_compare_fusion
  198.3 0.2 broadcast_and_fusion
  198.5 541.6 %all-to-all-done = f32[128,3,128,128]{3,2,1,0:T(8,128)} async-done(((f32[128,3,128,128]{3,2,1,0:T(8,128)}), f32[128,3,128,128]{3,2,1,0:T(8,128)}, u32[]{:S(2)}, u32[]{:S(2)}) %all-to-all-start) | async-done | bytes 25165856 | tf_op jit(solution)/shard_map/all_to_all | solution.py:34
  740.1 9.2 %reduce_sum.9 = f32[8,3,128,128]{3,2,1,0:T(8,128)S(1)} reduce(f32[16,8,3,128,128]{4,3,2,1,0:T(8,128)} %bitcast.16, f32[]{:T(128)} %constant.64.clone.1), dimensions={0}, to_apply=%region_0.2 | reduce | flops 5898240 | bytes 26738692 | tf_op jit(solution)/shard_map/reduce_sum | solution.py:37
  749.3 1.3 broadcast_select_fusion
  (5 shorter events, 0.1 us)
Async XLA Ops:
  6.5 103.2 %all-gather.2.cloned.1.call-start = ((), (), s32[]{:S(2)}) async-start(), calls=%async_computation.1 | async-start | bytes 13369344 | tf_op jit(solution)/shard_map/all_gather | solution.py:15
  190.1 8.1 %copy-start = (s32[8]{0:T(128)S(1)}, s32[8]{0:T(128)}, u32[]{:S(2)}) copy-start(s32[8]{0:T(128)} %param.11) | copy-start | bytes 100
  190.1 550.0 %all-to-all-start = ((f32[128,3,128,128]{3,2,1,0:T(8,128)}), f32[128,3,128,128]{3,2,1,0:T(8,128)}, u32[]{:S(2)}, u32[]{:S(2)}) async-start(f32[128,3,128,128]{3,2,1,0:T(8,128)} %fusion.24), calls=%async_computation | async-start | bytes 50331648 | tf_op jit(solution)/shard_map/all_to_all | solution.py:34
Sparse Core Ops, SparseCore 0:
  9.6 100.0 all-gather.1
where the time goes:
time: 758 us; the launch traced here: 757 us
  waiting for transfers between devices  642 us (85%)
  matrix products  43.2 us (6%)
  local copies, waits for them, and re-layouts  27.5 us (4%)
  other arithmetic  21.8 us (3%)
  between operations  14.8 us (2%)
  starting transfers between devices  8.13 us (1%)
    all_to_all x1, waiting for transfers between devices, per_device(): lax.all_to_all(partial_value, 'op', split_axis=0, concat_axis=0, tiled=True)  542 us
    all_gather x1, waiting for transfers between devices, per_device(): gathered = lax.all_gather(wavefunction, 'op', axis=0, tiled=True)  99.6 us
    dot_general x2, matrix products, per_device(): jnp.einsum('qvik,qlk->qvil', inner_block, right_env[slot_index], preferre...  43.2 us
    gather x2, local copies, waits for them, and re-layouts, per_device(): source = jnp.take(padded, row_index, axis=0)  26.1 us
  transfers between devices with their start and end apart: 2, of which 2 were waited for; matrix products, arithmetic and copies ran while one was open for 0% of the time, Pallas kernels for 0%

commit v1 on v0

--- a/solution.py
+++ b/solution.py
@@ -1,12 +1,260 @@
+import functools
+
 import jax
 import jax.numpy as jnp
 from jax import lax
+from jax.experimental import pallas as pl
+from jax.experimental.pallas import tpu as pltpu
 from jax.sharding import PartitionSpec as P
 
 TERMS = 32
-
-
-def per_device(wavefunction, left_env, right_env, term_shift, sector_width):
+MESH = pl.DeviceIdType.MESH
+
+
+def kernel(
+    n, slots, per,
+    shift_ref, wave_ref, left_ref, right_ref,
+    out_ref,
+    lbuf, rbuf, xbuf, sbuf, gbuf,
+    ag_send, ag_recv, rs_send, rs_recv, halo_send, halo_recv, env_local, env_send, env_recv, own_sem,
+):
+    half_ring = n // 2
+    half = per // 2
+    items = 2 * half_ring - 1
+    group = lax.axis_index("groups")
+    me = lax.axis_index("op")
+    c = lax.rem(me, 2)
+    chip = me // 2
+    row = lax.rem(chip, 2)
+    pos = (chip // 2) * (1 - row) + (n - 1 - chip // 2) * row
+
+    def wrap(r):
+        return lax.rem(r + 2 * n, n)
+
+    def chip_at(r):
+        side = r // half_ring
+        return (r * (1 - side) + (n - 1 - r) * side) * 2 + side
+
+    def ring_of(k):
+        side = lax.rem(k, 2)
+        return (k // 2) * (1 - side) + (n - 1 - k // 2) * side
+
+    def dev(r):
+        return (group, chip_at(r) * 2 + c)
+
+    sibling = (group, chip * 2 + 1 - c)
+    nexts = (dev(wrap(pos + 1)), dev(wrap(pos - 1)))
+    signs = (1, -1)
+
+    barrier = pltpu.get_barrier_semaphore()
+    for target in (nexts[0], nexts[1], sibling):
+        pl.semaphore_signal(barrier, inc=1, device_id=target, device_id_type=MESH)
+    pl.semaphore_wait(barrier, 3)
+
+    def half_of(d, k):
+        parity = lax.rem(k, 2)
+        return parity if d == 0 else 1 - parity
+
+    def ag_copy(d, k, r, h, src=None):
+        spot = xbuf.at[r, pl.ds(1 + h * half, half)]
+        return pltpu.make_async_remote_copy(
+            src_ref=spot if src is None else src, dst_ref=spot,
+            send_sem=ag_send.at[d, k], recv_sem=ag_recv.at[d, k],
+            device_id=nexts[d], device_id_type=MESH,
+        )
+
+    def halo_copy(r, h, src_row):
+        goal = ring_of(wrap(chip_at(r) - (1 - c) * (1 - h) + c * h))
+        return pltpu.make_async_remote_copy(
+            src_ref=src_row, dst_ref=xbuf.at[goal, (per + 1) * (1 - h)],
+            send_sem=halo_send.at[r, h], recv_sem=halo_recv.at[goal, h],
+            device_id=sibling, device_id_type=MESH,
+        )
+
+    def halo_arrival(r, h):
+        return pltpu.make_async_remote_copy(
+            src_ref=xbuf.at[r, (per + 1) * (1 - h)], dst_ref=xbuf.at[r, (per + 1) * (1 - h)],
+            send_sem=halo_send.at[r, h], recv_sem=halo_recv.at[r, h],
+            device_id=sibling, device_id_type=MESH,
+        )
+
+    def env_copies():
+        found = []
+        for e, (src, dst) in enumerate(((left_ref, lbuf), (right_ref, rbuf))):
+            mine = dst.at[pl.ds(c * slots, slots)]
+            found.append((
+                pltpu.make_async_copy(src.at[:, :, c], mine, env_local.at[e]),
+                pltpu.make_async_remote_copy(
+                    src_ref=src.at[:, :, 1 - c], dst_ref=mine,
+                    send_sem=env_send.at[e], recv_sem=env_recv.at[e],
+                    device_id=sibling, device_id_type=MESH,
+                ),
+                pltpu.make_async_remote_copy(
+                    src_ref=src.at[:, :, 1 - c], dst_ref=dst.at[pl.ds((1 - c) * slots, slots)],
+                    send_sem=env_send.at[e], recv_sem=env_recv.at[e],
+                    device_id=sibling, device_id_type=MESH,
+                ),
+            ))
+        return found
+
+    for k in range(2):
+        for d in range(2):
+            h = k if d == 0 else 1 - k
+            ag_copy(d, k, pos, h, wave_ref.at[pl.ds(h * half, half)]).start()
+    own = pltpu.make_async_copy(wave_ref, xbuf.at[pos, pl.ds(1, per)], own_sem.at[0])
+    own.start()
+    for h in range(2):
+        halo_copy(pos, h, wave_ref.at[h * (per - 1)]).start()
+    for local, remote, _ in env_copies():
+        local.start()
+        remote.start()
+
+    def gather_step(k, forward):
+        for d in range(2):
+            r = wrap(pos - signs[d] * (1 + k // 2))
+            h = half_of(d, k)
+            ag_copy(d, k, r, h).wait_recv()
+            if forward:
+                ag_copy(d, k + 2, r, h).start()
+            halo_copy(r, h, xbuf.at[r, 1 + h * (per - 1)]).start()
+
+    @pl.loop(0, items - 2)
+    def _(k):
+        gather_step(k, True)
+
+    @pl.loop(items - 2, items)
+    def _(k):
+        gather_step(k, False)
+
+    own.wait()
+    for local, remote, arrival in env_copies():
+        local.wait()
+        arrival.wait_recv()
+
+    @pl.loop(0, n)
+    def _(r):
+        for h in range(2):
+            halo_arrival(r, h).wait_recv()
+
+    xbuf[ring_of((n - 1) * c), (per + 1) * c] = jnp.zeros(xbuf.shape[2:], xbuf.dtype)
+
+    vectors = wave_ref.shape[1]
+    width = wave_ref.shape[2]
+
+    def product(r, sector):
+        k = chip_at(r)
+        lines = [[] for _ in range(vectors)]
+        rights = []
+        for t in range(2 * slots):
+            source = xbuf[r, sector + 2 - shift_ref[chip * 2 * slots + t]]
+            side = jnp.concatenate([source[v] for v in range(vectors)], axis=1)
+            inner = jnp.dot(lbuf[t, k, sector], side, preferred_element_type=jnp.float32)
+            inner = inner.astype(jnp.bfloat16)
+            for v in range(vectors):
+                lines[v].append(inner[:, v * width:(v + 1) * width])
+            rights.append(rbuf[t, k, sector])
+        inner = jnp.concatenate([jnp.concatenate(line, axis=1) for line in lines], axis=0)
+        total = lax.dot_general(
+            inner, jnp.concatenate(rights, axis=1), (((1,), (1,)), ((), ())),
+            preferred_element_type=jnp.float32,
+        )
+        return total.reshape((vectors, width, width))
+
+    def rs_copy(d, k):
+        return pltpu.make_async_remote_copy(
+            src_ref=sbuf.at[d, k], dst_ref=gbuf.at[d, k],
+            send_sem=rs_send.at[d, k], recv_sem=rs_recv.at[d, k],
+            device_id=nexts[d], device_id_type=MESH,
+        )
+
+    def scatter_step(k, add):
+        for d in range(2):
+            r = wrap(pos + signs[d] * (half_ring - (k + 1) // 2))
+            h = half_of(d, k)
+            if add:
+                rs_copy(d, k - 2).wait_recv()
+
+            @pl.loop(0, half)
+            def _(i):
+                total = product(r, h * half + i)
+                if add:
+                    total = total + gbuf[d, k - 2, i].astype(jnp.float32)
+                sbuf[d, k, i] = total.astype(jnp.bfloat16)
+
+            rs_copy(d, k).start()
+
+    @pl.loop(0, 2)
+    def _(k):
+        scatter_step(k, False)
+
+    @pl.loop(2, items)
+    def _(k):
+        scatter_step(k, True)
+
+    @pl.loop(0, per)
+    def _(i):
+        out_ref[i] = product(pos, i)
+
+    for k in range(items - 2, items):
+        for d in range(2):
+            h = k % 2 if d == 0 else 1 - k % 2
+            rs_copy(d, k).wait_recv()
+
+            @pl.loop(0, half)
+            def _(i):
+                out_ref[h * half + i] = out_ref[h * half + i] + gbuf[d, k, i].astype(jnp.float32)
+
+    @pl.loop(0, items)
+    def _(k):
+        for d in range(2):
+            ag_copy(d, k, wrap(pos - signs[d] * (k // 2)), half_of(d, k)).wait_send()
+            rs_copy(d, k).wait_send()
+
+    @pl.loop(0, n)
+    def _(r):
+        for h in range(2):
+            halo_copy(r, h, xbuf.at[r, 1 + h * (per - 1)]).wait_send()
+
+    for _, remote, _ in env_copies():
+        remote.wait_send()
+
+
+def ring_sum(wavefunction, left_env, right_env, term_shift):
+    n = lax.axis_size("op") // 2
+    slots = left_env.shape[0]
+    per, vectors, width, _ = wavefunction.shape
+    items = 2 * (n // 2) - 1
+    shaped = (slots, n, 2, per, width, width)
+    env = (2 * slots, n, per, width, width)
+    dma = pltpu.SemaphoreType.DMA
+    work = 2 * slots * n * per * vectors * width ** 3 * 4
+    return pl.pallas_call(
+        functools.partial(kernel, n, slots, per),
+        out_shape=jax.ShapeDtypeStruct(wavefunction.shape, jnp.float32),
+        in_specs=[
+            pl.BlockSpec(memory_space=pltpu.SMEM),
+            pl.BlockSpec(memory_space=pl.ANY),
+            pl.BlockSpec(memory_space=pl.ANY),
+            pl.BlockSpec(memory_space=pl.ANY),
+        ],
+        out_specs=pl.BlockSpec(memory_space=pltpu.VMEM),
+        scratch_shapes=[
+            pltpu.VMEM(env, jnp.bfloat16),
+            pltpu.VMEM(env, jnp.bfloat16),
+            pltpu.VMEM((n, per + 2, vectors, width, width), jnp.bfloat16),
+            pltpu.VMEM((2, items, per // 2, vectors, width, width), jnp.bfloat16),
+            pltpu.VMEM((2, items, per // 2, vectors, width, width), jnp.bfloat16),
+            dma((2, items)), dma((2, items)), dma((2, items)), dma((2, items)),
+            dma((n, 2)), dma((n, 2)), dma((2,)), dma((2,)), dma((2,)), dma((1,)),
+        ],
+        compiler_params=pltpu.CompilerParams(
+            collective_id=0, has_side_effects=True, vmem_limit_bytes=50 * 2 ** 20
+        ),
+        cost_estimate=pl.CostEstimate(flops=work, bytes_accessed=2 * left_env.size * 2, transcendentals=0),
+    )(term_shift, wavefunction, left_env.reshape(shaped), right_env.reshape(shaped))
+
+
+def gathered_sum(wavefunction, left_env, right_env, term_shift):
     devices = lax.axis_size("op")
     split_count = max(1, devices // TERMS)
     slot_dev = left_env.shape[0]
@@ -35,7 +283,14 @@
     per_peer = half_sec // devices
     grouped = arrived.reshape((split_count, devices // split_count, per_peer) + block_tail)
     summed = jnp.sum(grouped, axis=1)
-    summed = jnp.swapaxes(summed, 0, 1).reshape(wavefunction.shape)
+    return jnp.swapaxes(summed, 0, 1).reshape(wavefunction.shape)
+
+
+def per_device(wavefunction, left_env, right_env, term_shift, sector_width):
+    devices = lax.axis_size("op")
+    fits = devices <= TERMS and devices % 4 == 0 and devices >= 8 and wavefunction.shape[0] % 2 == 0
+    combine = ring_sum if fits else gathered_sum
+    summed = combine(wavefunction, left_env, right_env, term_shift)
     line_index = jnp.arange(wavefunction.shape[2], dtype=jnp.int32)
     widths = sector_width[:, None, None]
     keep_mask = (line_index[None, :, None] < widths) & (line_index[None, None, :] < widths)

time: 758 us -> 135 us (0.18)
  waiting for transfers between devices: 642 us -> 0 us
  Pallas kernels: 0 us -> 129 us
  matrix products: 43.2 us -> 0 us
  local copies, waits for them, and re-layouts: 27.5 us -> 1.78 us
  other arithmetic: 21.8 us -> 2.23 us
  between operations: 14.8 us -> 0.03 us
  starting transfers between devices: 8.13 us -> 0 us
    all_to_all x1 -> x0, waiting for transfers between devices: 542 us -> none  [per_device(): lax.all_to_all(partial_value, 'op', split_axis=0, concat_axis=0, tiled=True)]
    pallas_call x0 -> x1, Pallas kernels: none -> 129 us  [ring_sum(): pl.pallas_call(functools.partial(kernel, n, slots, per), out_shape=jax.Sh...]
    all_gather x1 -> x0, waiting for transfers between devices: 99.6 us -> none  [per_device(): gathered = lax.all_gather(wavefunction, 'op', axis=0, tiled=True)]
    dot_general x2 -> x0, matrix products: 43.2 us -> none  [per_device(): jnp.einsum('qvik,qlk->qvil', inner_block, right_env[slot_index], preferre...]
    gather x2 -> x0, local copies, waits for them, and re-layouts: 26.1 us -> none  [per_device(): source = jnp.take(padded, row_index, axis=0)]
    concatenate x1 -> x0, other arithmetic: 11.1 us -> none  [per_device(): padded = jnp.concatenate([zero_block, gathered, zero_block], axis=0)]
    reduce_sum x1 -> x0, other arithmetic: 9.16 us -> none  [per_device(): summed = jnp.sum(grouped, axis=1)]
    all_to_all x1 -> x0, starting transfers between devices: 8.13 us -> none  [per_device(): lax.all_to_all(partial_value, 'op', split_axis=0, concat_axis=0, tiled=True)]
  transfers between devices with their start and end apart: 2 -> 0, of which waited for: 2 -> 0; matrix products, arithmetic and copies ran while one was open for 0% -> 0% of each run, Pallas kernels for 0% -> 0%
where the time goes in v1:
time: 135 us; the launch traced here: 133 us
  Pallas kernels  129 us (96%)
  other arithmetic  2.23 us (2%)
  local copies, waits for them, and re-layouts  1.78 us (1%)
    pallas_call x1, Pallas kernels, ring_sum(): pl.pallas_call(functools.partial(kernel, n, slots, per), out_shape=jax.Sh...  129 us

profile of v1, /device:TPU:13, one launch (start us, length us, event | category | flops | bytes accessed | tf_op | source)
XLA Modules:
  0.0 132.8 jit_solution(2640299118881927920)
XLA Ops:
  0.0 0.7 iota_compare_fusion
  0.7 0.2 broadcast_and_fusion
  0.9 0.0 copy-start
  1.0 1.1 copy-done
  2.1 0.0 copy-start.1
  2.1 0.7 copy-done.1
  2.7 128.8 %shard_map.55 = f32[8,3,128,128]{3,2,1,0:T(8,128)S(1)} custom-call(s32[32]{0:T(128)S(1)} %copy-done.1, bf16[8,3,128,128]{3,2,1,0:T(8,128)(2,1)S(1)} %copy-done, bf16[2,8,2,8,128,128]{5,4,3,2,1,0:T(8,128)(2,1)} %bitcast.2, bf16[2,8,2,8,128,128]{5,4,3,2,1,0:T(8,128)(2,1)} %bitcast.3), custom_call_target="tpu_custom_call" | custom-call | flops 6442450944 | bytes 16777216 | tf_op jit(solution)/shard_map/pallas_call | solution.py:231
  131.5 1.3 broadcast_select_fusion
Async XLA Ops:
  0.9 1.1 copy-start
  2.1 0.7 copy-start.1

commit v2 on v1

--- a/solution.py
+++ b/solution.py
@@ -13,10 +13,11 @@
 
 def kernel(
     n, slots, per,
-    shift_ref, wave_ref, left_ref, right_ref,
+    shift_ref, live_ref, wave_ref, left_ref, right_ref,
     out_ref,
     lbuf, rbuf, xbuf, sbuf, gbuf,
     ag_send, ag_recv, rs_send, rs_recv, halo_send, halo_recv, env_local, env_send, env_recv, own_sem,
+    head_send, head_recv,
 ):
     half_ring = n // 2
     half = per // 2
@@ -52,7 +53,7 @@
     pl.semaphore_wait(barrier, 3)
 
     def half_of(d, k):
-        parity = lax.rem(k, 2)
+        parity = k % 2 if isinstance(k, int) else lax.rem(k, 2)
         return parity if d == 0 else 1 - parity
 
     def ag_copy(d, k, r, h, src=None):
@@ -171,7 +172,11 @@
         for d in range(2):
             r = wrap(pos + signs[d] * (half_ring - (k + 1) // 2))
             h = half_of(d, k)
-            if add:
+            if isinstance(k, int) and k == 2:
+                @pl.loop(0, half)
+                def _(i):
+                    head_copy(d, i).wait_recv()
+            elif add:
                 rs_copy(d, k - 2).wait_recv()
 
             @pl.loop(0, half)
@@ -183,11 +188,24 @@
 
             rs_copy(d, k).start()
 
-    @pl.loop(0, 2)
-    def _(k):
-        scatter_step(k, False)
-
-    @pl.loop(2, items)
+    def head_copy(d, i):
+        return pltpu.make_async_remote_copy(
+            src_ref=sbuf.at[d, 0, i], dst_ref=gbuf.at[d, 0, i],
+            send_sem=head_send.at[d, i], recv_sem=head_recv.at[d, i],
+            device_id=nexts[d], device_id_type=MESH,
+        )
+
+    @pl.loop(0, half)
+    def _(i):
+        for d in range(2):
+            r = wrap(pos + signs[d] * half_ring)
+            sbuf[d, 0, i] = product(r, d * half + i).astype(jnp.bfloat16)
+            head_copy(d, i).start()
+
+    scatter_step(1, False)
+    scatter_step(2, True)
+
+    @pl.loop(3, items)
     def _(k):
         scatter_step(k, True)
 
@@ -202,13 +220,29 @@
 
             @pl.loop(0, half)
             def _(i):
-                out_ref[h * half + i] = out_ref[h * half + i] + gbuf[d, k, i].astype(jnp.float32)
+                value = out_ref[h * half + i] + gbuf[d, k, i].astype(jnp.float32)
+                if k == items - 1:
+                    live = live_ref[h * half + i]
+                    down = lax.broadcasted_iota(jnp.int32, (width, width), 0)
+                    along = lax.broadcasted_iota(jnp.int32, (width, width), 1)
+                    keep = ((down < live) & (along < live))[None]
+                    value = jnp.where(keep, value, jnp.float32(0.0))
+                out_ref[h * half + i] = value
 
     @pl.loop(0, items)
     def _(k):
         for d in range(2):
             ag_copy(d, k, wrap(pos - signs[d] * (k // 2)), half_of(d, k)).wait_send()
+
+    @pl.loop(1, items)
+    def _(k):
+        for d in range(2):
             rs_copy(d, k).wait_send()
+
+    @pl.loop(0, half)
+    def _(i):
+        for d in range(2):
+            head_copy(d, i).wait_send()
 
     @pl.loop(0, n)
     def _(r):
@@ -219,7 +253,7 @@
         remote.wait_send()
 
 
-def ring_sum(wavefunction, left_env, right_env, term_shift):
+def ring_sum(wavefunction, left_env, right_env, term_shift, sector_width):
     n = lax.axis_size("op") // 2
     slots = left_env.shape[0]
     per, vectors, width, _ = wavefunction.shape
@@ -232,6 +266,7 @@
         functools.partial(kernel, n, slots, per),
         out_shape=jax.ShapeDtypeStruct(wavefunction.shape, jnp.float32),
         in_specs=[
+            pl.BlockSpec(memory_space=pltpu.SMEM),
             pl.BlockSpec(memory_space=pltpu.SMEM),
             pl.BlockSpec(memory_space=pl.ANY),
             pl.BlockSpec(memory_space=pl.ANY),
@@ -246,12 +281,13 @@
             pltpu.VMEM((2, items, per // 2, vectors, width, width), jnp.bfloat16),
             dma((2, items)), dma((2, items)), dma((2, items)), dma((2, items)),
             dma((n, 2)), dma((n, 2)), dma((2,)), dma((2,)), dma((2,)), dma((1,)),
+            dma((2, per // 2)), dma((2, per // 2)),
         ],
         compiler_params=pltpu.CompilerParams(
-            collective_id=0, has_side_effects=True, vmem_limit_bytes=50 * 2 ** 20
+            collective_id=0, has_side_effects=True, vmem_limit_bytes=60 * 2 ** 20
         ),
         cost_estimate=pl.CostEstimate(flops=work, bytes_accessed=2 * left_env.size * 2, transcendentals=0),
-    )(term_shift, wavefunction, left_env.reshape(shaped), right_env.reshape(shaped))
+    )(term_shift, sector_width, wavefunction, left_env.reshape(shaped), right_env.reshape(shaped))
 
 
 def gathered_sum(wavefunction, left_env, right_env, term_shift):
@@ -289,8 +325,9 @@
 def per_device(wavefunction, left_env, right_env, term_shift, sector_width):
     devices = lax.axis_size("op")
     fits = devices <= TERMS and devices % 4 == 0 and devices >= 8 and wavefunction.shape[0] % 2 == 0
-    combine = ring_sum if fits else gathered_sum
-    summed = combine(wavefunction, left_env, right_env, term_shift)
+    if fits:
+        return ring_sum(wavefunction, left_env, right_env, term_shift, sector_width)
+    summed = gathered_sum(wavefunction, left_env, right_env, term_shift)
     line_index = jnp.arange(wavefunction.shape[2], dtype=jnp.int32)
     widths = sector_width[:, None, None]
     keep_mask = (line_index[None, :, None] < widths) & (line_index[None, None, :] < widths)

time: 135 us -> 133 us (0.985)
  other arithmetic: 2.23 us -> 0 us
    unnamed x4 -> x1, local copies, waits for them, and re-layouts: 1.78 us -> 2.7 us
where the time goes in v2:
time: 133 us; the launch traced here: 131 us
  Pallas kernels  128 us (96%)
  local copies, waits for them, and re-layouts  2.7 us (2%)
    pallas_call x1, Pallas kernels, ring_sum(): pl.pallas_call(functools.partial(kernel, n, slots, per), out_shape=jax.Sh...  128 us
    unnamed x1, local copies, waits for them, and re-layouts  2.7 us

profile of v2, /device:TPU:13, one launch (start us, length us, event | category | flops | bytes accessed | tf_op | source)
XLA Modules:
  0.0 131.2 jit_solution(16893679310477383715)
XLA Ops:
  0.0 128.5 %shard_map.55 = f32[8,3,128,128]{3,2,1,0:T(8,128)} custom-call(s32[32]{0:T(128)} %shift_ref.1, s32[8]{0:T(128)} %live_ref.1, bf16[8,3,128,128]{3,2,1,0:T(8,128)(2,1)} %wave_ref.1, bf16[2,8,2,8,128,128]{5,4,3,2,1,0:T(8,128)(2,1)} %bitcast.2, bf16[2,8,2,8,128,128]{5,4,3,2,1,0:T(8,128)(2,1)} %bitcast.3), custom_call_target="tpu_custom_call" | custom-call | flops 6442450944 | bytes 16777216 | tf_op jit(solution)/shard_map/pallas_call | solution.py:265
  128.5 2.7 %copy.7 = f32[8,3,128,128]{3,2,1,0:T(8,128)} copy(f32[8,3,128,128]{3,2,1,0:T(8,128)} %shard_map.55) | data formatting | bytes 3145728

commit v3 on v2

--- a/solution.py
+++ b/solution.py
@@ -268,9 +268,9 @@
         in_specs=[
             pl.BlockSpec(memory_space=pltpu.SMEM),
             pl.BlockSpec(memory_space=pltpu.SMEM),
-            pl.BlockSpec(memory_space=pl.ANY),
-            pl.BlockSpec(memory_space=pl.ANY),
-            pl.BlockSpec(memory_space=pl.ANY),
+            pl.BlockSpec(memory_space=pltpu.HBM),
+            pl.BlockSpec(memory_space=pltpu.HBM),
+            pl.BlockSpec(memory_space=pltpu.HBM),
         ],
         out_specs=pl.BlockSpec(memory_space=pltpu.VMEM),
         scratch_shapes=[
@@ -284,7 +284,7 @@
             dma((2, per // 2)), dma((2, per // 2)),
         ],
         compiler_params=pltpu.CompilerParams(
-            collective_id=0, has_side_effects=True, vmem_limit_bytes=60 * 2 ** 20
+            collective_id=0, has_side_effects=True, vmem_limit_bytes=48 * 2 ** 20
         ),
         cost_estimate=pl.CostEstimate(flops=work, bytes_accessed=2 * left_env.size * 2, transcendentals=0),
     )(term_shift, sector_width, wavefunction, left_env.reshape(shaped), right_env.reshape(shaped))

time: 133 us -> 132 us (level)
    pallas_call x1, Pallas kernels: 128 us -> 127 us  [ring_sum(): pl.pallas_call(functools.partial(kernel, n, slots, per), out_shape=jax.Sh...]
    unnamed x1 -> x7, local copies, waits for them, and re-layouts: 2.7 us -> 3.59 us
where the time goes in v3:
time: 132 us; the launch traced here: 131 us
  Pallas kernels  127 us (96%)
  local copies, waits for them, and re-layouts  3.59 us (3%)
    pallas_call x1, Pallas kernels, ring_sum(): pl.pallas_call(functools.partial(kernel, n, slots, per), out_shape=jax.Sh...  127 us
    unnamed x7, local copies, waits for them, and re-layouts  3.59 us

profile of v3, /device:TPU:13, one launch (start us, length us, event | category | flops | bytes accessed | tf_op | source)
XLA Modules:
  0.0 130.6 jit_solution(14460328063802078146)
XLA Ops:
  0.0 0.0 copy-start
  0.0 1.1 copy-done
  1.1 0.0 copy-start.1
  1.1 0.7 copy-done.1
  1.8 0.0 copy-start.2
  1.8 0.7 copy-done.2
  2.4 127.0 %shard_map.55 = f32[8,3,128,128]{3,2,1,0:T(8,128)S(1)} custom-call(s32[32]{0:T(128)S(1)} %copy-done.1, s32[8]{0:T(128)S(1)} %copy-done.2, bf16[8,3,128,128]{3,2,1,0:T(8,128)(2,1)S(1)} %copy-done, bf16[2,8,2,8,128,128]{5,4,3,2,1,0:T(8,128)(2,1)} %bitcast.2, bf16[2,8,2,8,128,128]{5,4,3,2,1,0:T(8,128)(2,1)} %bitcast.3), custom_call_target="tpu_custom_call" | custom-call | flops 6442450944 | bytes 16777216 | tf_op jit(solution)/shard_map/pallas_call | solution.py:265
  129.5 1.1 copy.7
Async XLA Ops:
  0.0 1.1 copy-start
  1.1 0.7 copy-start.1
  1.8 0.7 copy-start.2

commit v4 on v3

--- a/solution.py
+++ b/solution.py
@@ -195,7 +195,7 @@
             device_id=nexts[d], device_id_type=MESH,
         )
 
-    @pl.loop(0, half)
+    @pl.loop(0, half, unroll=True)
     def _(i):
         for d in range(2):
             r = wrap(pos + signs[d] * half_ring)

time: 132 us -> 132 us (level)
  no operation moved by 1% of the time
where the time goes in v4:
time: 132 us; the launch traced here: 131 us
  Pallas kernels  127 us (96%)
  local copies, waits for them, and re-layouts  3.59 us (3%)
    pallas_call x1, Pallas kernels, ring_sum(): pl.pallas_call(functools.partial(kernel, n, slots, per), out_shape=jax.Sh...  127 us
    unnamed x7, local copies, waits for them, and re-layouts  3.59 us

profile of v4, /device:TPU:13, one launch (start us, length us, event | category | flops | bytes accessed | tf_op | source)
XLA Modules:
  0.0 130.6 jit_solution(15439612657598841242)
XLA Ops:
  0.0 0.0 copy-start
  0.0 1.1 copy-done
  1.1 0.0 copy-start.1
  1.1 0.7 copy-done.1
  1.8 0.0 copy-start.2
  1.8 0.7 copy-done.2
  2.4 127.0 %shard_map.55 = f32[8,3,128,128]{3,2,1,0:T(8,128)S(1)} custom-call(s32[32]{0:T(128)S(1)} %copy-done.1, s32[8]{0:T(128)S(1)} %copy-done.2, bf16[8,3,128,128]{3,2,1,0:T(8,128)(2,1)S(1)} %copy-done, bf16[2,8,2,8,128,128]{5,4,3,2,1,0:T(8,128)(2,1)} %bitcast.2, bf16[2,8,2,8,128,128]{5,4,3,2,1,0:T(8,128)(2,1)} %bitcast.3), custom_call_target="tpu_custom_call" | custom-call | flops 6442450944 | bytes 16777216 | tf_op jit(solution)/shard_map/pallas_call | solution.py:265
  129.5 1.1 copy.7
Async XLA Ops:
  0.0 1.1 copy-start
  1.1 0.7 copy-start.1
  1.8 0.7 copy-start.2
